TPU v7x, 32 devices: a whole 2x2x4 slice. The times are simulated.
32 devices in a mesh: dp: 4 (over z), table: 8 (over y, x, core).
Axes of the slice: x: 2, y: 2, z: 4, core: 2. Of those that a mesh axis runs over, the one named last changes fastest.
Arguments:
- table: bfloat16 [32768, 512], P('table'), may hold values from -6 to 6
- w_in: bfloat16 [512, 2048], replicated, may hold values from -0.25 to 0.25
- w_out: bfloat16 [512, 512], replicated, may hold values from -0.25 to 0.25
- owner: int32 [32768, 2], P(('dp', 'table')), may hold values from 0 to 7, all different within a row; in each aligned block of 1024 rows (0 to 1023, 1024 to 2047, ...) at most 512 rows name the same one
- local_row: int32 [32768, 2], P(('dp', 'table')), may hold values from 0 to 4095
- doc_ids: int32 [32, 1024], P(('dp', 'table')), may hold values from 0 to 3, never falling along the last dimension, each value on 1 to 768 neighbouring positions
- out_grad: bfloat16 [32768, 512], P(('dp', 'table')), may hold values from -6 to 6
Outputs:
- layer_out: bfloat16 [32768, 512], P(('dp', 'table'))
- grad_w_in: float32 [512, 2048], replicated
- grad_w_out: float32 [512, 512], replicated
- grad_table: float32 [32768, 512], P('table', 'dp')
Inputs may be any that keep to these rules, and one draw needn't show every extreme that they name: The 2 owners of one event differ; among the events of one block of 1024, no owner is named by more than 512 lookups. `doc_ids`: along a row the ids never fall; every id of 0 to 3 covers 1 to 768 events.
All inputs are finite; a program needn't handle non-finite values.
Results may differ from a plain program's by a relative error of at most 0.014.
Values may be sent and summed in bfloat16 or wider, within the bound.
A program may use at most 128 MiB of HBM per device.

v0:
```python
import jax
import jax.numpy as jnp
from jax import lax
from jax.sharding import PartitionSpec as P

HEADS = 4
MAXLEN = 768


def normalize(values):
    center = values - jnp.mean(values, axis=-1, keepdims=True)
    spread = jnp.mean(center * center, axis=-1, keepdims=True)
    return center * lax.rsqrt(spread + 1e-06)


def hstu_layer(inputs, w_in, w_out, segment):
    length, width = inputs.shape
    head_dim = width // HEADS
    widened = inputs.astype(jnp.float32)
    normed = normalize(widened).astype(jnp.bfloat16)
    projected = jax.nn.silu(jnp.dot(normed, w_in, preferred_element_type=jnp.float32)).astype(
        jnp.bfloat16
    )
    gate_part, value_part, query_part, key_part = jnp.split(projected, 4, axis=1)
    query_heads = query_part.reshape(length, HEADS, head_dim)
    key_heads = key_part.reshape(length, HEADS, head_dim)
    value_heads = value_part.reshape(length, HEADS, head_dim)
    scores = jnp.einsum(
        "thd,shd->hts", query_heads, key_heads, preferred_element_type=jnp.float32
    ) * head_dim ** (-0.5)
    row_index = lax.broadcasted_iota(jnp.int32, (length, length), 0)
    col_index = lax.broadcasted_iota(jnp.int32, (length, length), 1)
    allowed = (segment[:, None] == segment[None, :]) & (row_index >= col_index)
    weights = (jnp.where(allowed[None], jax.nn.silu(scores), 0.0) / MAXLEN).astype(jnp.bfloat16)
    mixed = jnp.einsum(
        "hts,shd->thd", weights, value_heads, preferred_element_type=jnp.float32
    ).reshape(length, width)
    gated = (normalize(mixed) * gate_part.astype(jnp.float32)).astype(jnp.bfloat16)
    return (widened + jnp.dot(gated, w_out, preferred_element_type=jnp.float32)).astype(
        jnp.bfloat16
    )


def shards(table, w_in, w_out, owner, local_row, doc_ids, out_grad):
    events, lookups_each = owner.shape
    width = table.shape[1]
    rows_owned = table.shape[0]
    owners = lax.axis_size("table")
    capacity = 2 * events * lookups_each // owners
    lookups = events * lookups_each
    flat_owner = owner.reshape(lookups)
    flat_local = local_row.reshape(lookups)
    member = (flat_owner[:, None] == jnp.arange(owners, dtype=jnp.int32)[None, :]).astype(jnp.int32)
    position = jnp.sum(jnp.cumsum(member, axis=0) * member, axis=1) - 1
    slot_index = flat_owner * capacity + position
    requests = (
        jnp.zeros((owners * capacity,), jnp.int32)
        .at[slot_index]
        .set(flat_local)
        .reshape(owners, capacity)
    )
    found = jnp.take(
        table, lax.all_to_all(requests, "table", split_axis=0, concat_axis=0, tiled=True), axis=0
    )
    arrived = lax.all_to_all(found, "table", split_axis=0, concat_axis=0, tiled=True)
    picked = jnp.take(arrived.reshape(owners * capacity, width), slot_index, axis=0)
    embedded = jnp.sum(
        picked.astype(jnp.float32).reshape(events, lookups_each, width), axis=1
    ).astype(jnp.bfloat16)
    segment = doc_ids[0]

    def forward(first, second, third):
        return hstu_layer(first, second, third, segment)

    layer_out, pullback = jax.vjp(forward, embedded, w_in, w_out)
    embed_grad, grad_first, grad_second = pullback(out_grad)
    grad_w_in, grad_w_out = lax.psum(
        (grad_first.astype(jnp.float32), grad_second.astype(jnp.float32)), ("dp", "table")
    )
    per_lookup = jnp.broadcast_to(embed_grad[:, None, :], (events, lookups_each, width)).reshape(
        lookups, width
    )
    sending = (
        jnp.zeros((owners * capacity, width), jnp.bfloat16)
        .at[slot_index]
        .set(per_lookup)
        .reshape(owners, capacity, width)
    )
    received, received_ids = (
        lax.all_to_all(sending, "table", split_axis=0, concat_axis=0, tiled=True),
        lax.all_to_all(requests, "table", split_axis=0, concat_axis=0, tiled=True),
    )
    summed = jax.ops.segment_sum(
        received.reshape(owners * capacity, width).astype(jnp.float32),
        received_ids.reshape(-1),
        num_segments=rows_owned,
    )
    grad_table = lax.psum_scatter(
        summed.astype(jnp.bfloat16), "dp", scatter_dimension=1, tiled=True
    ).astype(jnp.float32)
    return (layer_out, grad_w_in, grad_w_out, grad_table)


def solution(mesh):
    placed = (
        P("table", None),
        P(),
        P(),
        P(("dp", "table"), None),
        P(("dp", "table"), None),
        P(("dp", "table"), None),
        P(("dp", "table"), None),
    )
    return jax.shard_map(
        shards,
        mesh=mesh,
        in_specs=placed,
        out_specs=(P(("dp", "table"), None), P(), P(), P("table", "dp")),
        check_vma=False,
    )
```

profile of v0, /device:TPU:0, one launch (start us, length us, event | category | flops | bytes accessed | tf_op | source)
XLA Modules:
  0.0 576.1 jit_solution(3755238952161310112)
XLA Ops:
  15.0 8.1 %scatter_custom_fusion = s32[4096]{0:T(1024)S(1)} fusion(s32[2048]{0:T(1024)S(1)} %bitcast.117, s32[2048]{0:T(1024)S(1)} %reshape.282, s32[]{:T(128)} %constant.61.clone.1), kind=kCustom, calls=%fused_computation.88 | custom fusion | bytes 16388 | tf_op jit(solution)/shard_map/scatter | solution.py:59
  23.1 9.7 %all_to_all.26 = s32[8,1,512]{2,1,0:T(1,128)S(1)} all-to-all(s32[8,1,512]{2,1,0:T(1,128)S(1)} %bitcast.115), channel_id=1, replica_groups=mesh['dp'=4,'table'=8] {'table'}, dimensions={0} | all-to-all | bytes 32768 | tf_op jit(solution)/shard_map/all_to_all | solution.py:63
  32.8 20.2 %gather_fusion = bf16[4096,512]{1,0:T(8,128)(2,1)} fusion(bf16[4096,512]{1,0:T(8,128)(2,1)} %param.7, s32[4096]{0:T(1024)S(1)} %broadcast_clamp_fusion), kind=kCustom, calls=%fused_computation | custom fusion | bytes 8404992 | tf_op jit(solution)/shard_map/jit(_take)/gather | solution.py:62
  57.0 4.7 all-to-all-start.1
  64.7 46.0 %all-to-all-done.1 = bf16[8,512,512]{2,1,0:T(8,128)(2,1)} async-done(((bf16[8,512,512]{2,1,0:T(8,128)(2,1)}), bf16[8,512,512]{2,1,0:T(8,128)(2,1)}, u32[]{:S(2)}, u32[]{:S(2)}) %all-to-all-start.1) | async-done | bytes 4194336 | tf_op jit(solution)/shard_map/all_to_all | solution.py:65
  110.8 12.0 %gather_fusion.1 = bf16[2048,512]{1,0:T(8,128)(2,1)} fusion(bf16[4096,512]{1,0:T(8,128)(2,1)} %bitcast.7, s32[2048]{0:T(1024)S(1)} %broadcast_clamp_fusion.1), kind=kCustom, calls=%fused_computation.1 | custom fusion | bytes 4202496 | tf_op jit(solution)/shard_map/jit(_take)/gather | solution.py:66
  126.9 9.6 %fusion.20 = bf16[1024,512]{1,0:T(8,128)(2,1)S(1)} fusion(bf16[1024,2,512]{2,1,0:T(2,128)(2,1)} %gather.12, pred[1024,2]{1,0:T(8,128)(4,1)S(1)} %copy.65), kind=kLoop, calls=%fused_computation.46 | loop fusion | flops 1572864 | bytes 3147776 | tf_op jit(solution)/shard_map/reduce_sum | solution.py:67
  137.3 5.7 multiply_convert_fusion.1
  151.4 12.3 %multiply_convert_fusion = (bf16[4,1024,1024]{2,1,0:T(8,128)(2,1)S(1)}, f32[4,1024,1024]{2,1,0:T(8,128)}) fusion(pred[1024,1024]{1,0:T(8,128)(4,1)} %fusion.8, bf16[1024,4,128]{0,2,1:T(8,128)(2,1)} %bitcast.106, bf16[1024,4,128]{0,2,1:T(8,128)(2,1)} %bitcast.108), kind=kOutput, calls=%fused_computation.9 | convolution fusion | flops 1107296256 | bytes 28311552 | tf_op jit(solution)/shard_map/jvp(thd,shd->hts)/dot_general | solution.py:28
  178.3 6.1 %fusion.28 = bf16[4,128,1024]{2,1,0:T(8,128)(2,1)} fusion(bf16[4,1024,1024]{2,1,0:T(8,128)(2,1)} %copy-done.1, f32[1024,512]{1,0:T(8,128)S(1)} %get-tuple-element.7, f32[1024]{0:T(1024)S(1)} %negate_multiply_fusion.1), kind=kOutput, calls=%fused_computation.60 | convolution fusion | flops 1074790400 | bytes 11538432 | tf_op jit(solution)/shard_map/transpose(jvp(hts,shd->thd))/dot_general | solution.py:35
  184.4 15.0 %fusion.2 = bf16[4,1024,1024]{2,1,0:T(8,128)(2,1)} fusion(f32[4,1024,1024]{2,1,0:T(8,128)} %get-tuple-element.18, pred[1024,1024]{1,0:T(8,128)(4,1)S(1)} %copy-done.10, bf16[128,4,8,128]{3,2,1,0:T(8,128)(2,1)S(1)} %copy-done.9, f32[1024,512]{1,0:T(8,128)S(1)} %get-tuple-element.7, f32[1024]{0:T(1024)S(1)} %negate_multiply_fusion.1), kind=kOutput, calls=%fused_computation.8 | convolution fusion | flops 1137704960 | bytes 29364224 | tf_op jit(solution)/shard_map/transpose(jvp(hts,shd->thd))/dot_general | solution.py:35
  199.4 7.4 %fusion.49 = bf16[4,1024,128]{1,2,0:T(8,128)(2,1)} fusion(bf16[4,1024,1024]{2,1,0:T(8,128)(2,1)} %fusion.2, bf16[1024,4,128]{0,2,1:T(8,128)(2,1)S(1)} %bitcast.109), kind=kOutput, calls=%fused_computation.107 | convolution fusion | flops 1073741824 | bytes 10485760 | tf_op jit(solution)/shard_map/transpose(jvp(thd,shd->hts))/dot_general | solution.py:28
  206.8 5.7 fusion.48
  219.4 6.5 %fusion.3 = bf16[1024,2048]{1,0:T(8,128)(2,1)S(1)} fusion(f32[1024,2048]{1,0:T(8,128)} %get-tuple-element.16, bf16[1024,512]{1,0:T(8,128)(2,1)} %copy.90, bf16[1024,512]{1,0:T(8,128)(2,1)} %copy.89, bf16[1024,512]{1,0:T(8,128)(2,1)} %copy.88, bf16[1024,512]{1,0:T(8,128)(2,1)} %get-tuple-element.12), kind=kLoop, calls=%fused_computation.14 | loop fusion | flops 37748736 | bytes 16777216 | tf_op jit(solution)/shard_map/transpose(jvp(jit(silu)))/add_any | solution.py:21
  232.8 4.1 reshape.290
  237.0 12.8 %scatter_custom_fusion.1 = bf16[4096,512]{1,0:T(8,128)(2,1)} fusion(s32[2048]{0:T(1024)S(1)} %bitcast.119, bf16[2048,512]{1,0:T(8,128)(2,1)} %reshape.290, bf16[]{:T(256)} %constant.66.clone.1), kind=kCustom, calls=%fused_computation.53 | custom fusion | bytes 4194816 | tf_op jit(solution)/shard_map/scatter | solution.py:86
  249.8 53.6 %all_to_all.27 = bf16[8,512,512]{2,1,0:T(8,128)(2,1)} all-to-all(bf16[8,512,512]{2,1,0:T(8,128)(2,1)} %bitcast.103), channel_id=1, replica_groups=mesh['dp'=4,'table'=8] {'table'}, dimensions={0} | all-to-all | bytes 8388608 | tf_op jit(solution)/shard_map/all_to_all | solution.py:90
  303.4 31.7 %scatter_custom_fusion.2 = f32[4096,512]{1,0:T(8,128)} fusion(s32[4096]{0:T(1024)S(1)} %bitcast.113, bf16[4096,512]{1,0:T(8,128)(2,1)} %bitcast.104, f32[]{:T(128)} %constant.67.clone.1), kind=kCustom, calls=%fused_computation.16 | custom fusion | flops 4194304 | bytes 12582916 | tf_op jit(solution)/shard_map/scatter-add | solution.py:93
  335.1 5.9 %convert_element_type.131 = bf16[4096,512]{1,0:T(8,128)(2,1)} convert(f32[4096,512]{1,0:T(8,128)} %scatter_custom_fusion.2) | non-fusion elementwise | flops 2097152 | bytes 12582912 | tf_op jit(solution)/shard_map/convert_element_type | solution.py:99
  341.0 6.4 %copy.91 = bf16[4096,512]{0,1:T(8,128)(2,1)} copy(bf16[4096,512]{1,0:T(8,128)(2,1)} %convert_element_type.131) | data formatting | bytes 8388608
  350.9 4.6 fusion.13
  358.6 72.9 %reduce-scatter.4.cloned.1.call-done = bf16[128,4096]{1,0:T(8,128)(2,1)} async-done(((bf16[512,4096]{1,0:T(8,128)(2,1)}), bf16[128,4096]{1,0:T(8,128)(2,1)}) %reduce-scatter.4.cloned.1.call-update) | async-done | bytes 1048592
  434.5 127.9 %all-reduce.3.cloned.1.call-done = (f32[512,2048]{1,0:T(8,128)}, f32[512,512]{1,0:T(8,128)}) async-done(((f32[512,2048]{1,0:T(8,128)}, f32[512,512]{1,0:T(8,128)}), (f32[512,2048]{1,0:T(8,128)}, f32[512,512]{1,0:T(8,128)})) %all-reduce.3.cloned.1.call-update) | async-done | bytes 5242896 | tf_op jit(solution)/shard_map/psum | solution.py:77
  562.5 4.8 copy.125
  (92 shorter events, 66.2 us)
Async XLA Ops:
  8.0 129.3 %copy-start = (bf16[512,2048]{1,0:T(8,128)(2,1)S(1)}, bf16[512,2048]{1,0:T(8,128)(2,1)}, u32[]{:S(2)}) copy-start(bf16[512,2048]{1,0:T(8,128)(2,1)} %param.8) | copy-start | bytes 6291460
  57.0 5.9 %copy-start.14 = (s32[1024,2]{0,1:T(2,128)S(1)}, s32[1024,2]{0,1:T(2,128)}, u32[]{:S(2)}) copy-start(s32[1024,2]{0,1:T(2,128)} %param.10) | copy-start | bytes 24580
  57.0 6.2 %copy-start.15 = (s32[1,1024]{1,0:T(1,128)S(1)}, s32[1,1024]{1,0:T(1,128)}, u32[]{:S(2)}) copy-start(s32[1,1024]{1,0:T(1,128)} %param.12) | copy-start | bytes 12292
  57.0 53.8 %all-to-all-start.1 = ((bf16[8,512,512]{2,1,0:T(8,128)(2,1)}), bf16[8,512,512]{2,1,0:T(8,128)(2,1)}, u32[]{:S(2)}, u32[]{:S(2)}) async-start(bf16[8,512,512]{2,1,0:T(8,128)(2,1)} %broadcast_select_fusion), calls=%async_computation.1 | async-start | bytes 8388608 | tf_op jit(solution)/shard_map/all_to_all | solution.py:65
  61.7 369.8 %reduce-scatter.4.cloned.1.call-start = ((), (), s32[]{:S(2)}) async-start(), calls=%async_computation.4 | async-start | bytes 5242880
  142.9 2.0 copy-start.6
  151.4 12.3 %copy-start.8 = (bf16[128,4,8,128]{3,2,1,0:T(8,128)(2,1)S(1)}, bf16[128,4,8,128]{3,2,1,0:T(8,128)(2,1)}, u32[]{:S(2)}) copy-start(bf16[128,4,8,128]{3,2,1,0:T(8,128)(2,1)} %get-tuple-element.9) | copy-start | bytes 3145732
  163.7 3.2 copy-start.1
  166.9 1.3 copy-start.5
  171.4 3.4 copy-start.4
  178.3 6.1 %copy-start.9 = (bf16[128,4,8,128]{3,2,1,0:T(8,128)(2,1)S(1)}, bf16[128,4,8,128]{3,2,1,0:T(8,128)(2,1)}, u32[]{:S(2)}) copy-start(bf16[128,4,8,128]{3,2,1,0:T(8,128)(2,1)} %get-tuple-element.9) | copy-start | bytes 3145732
  178.3 6.1 %copy-start.10 = (pred[1024,1024]{1,0:T(8,128)(4,1)S(1)}, pred[1024,1024]{1,0:T(8,128)(4,1)}, u32[]{:S(2)}) copy-start(pred[1024,1024]{1,0:T(8,128)(4,1)} %fusion.8) | copy-start | bytes 3145732
  184.4 15.0 %copy-start.12 = (bf16[1024,512]{0,1:T(8,128)(2,1)S(1)}, bf16[1024,512]{0,1:T(8,128)(2,1)}, u32[]{:S(2)}) copy-start(bf16[1024,512]{0,1:T(8,128)(2,1)} %copy.95) | copy-start | bytes 3145732
  199.4 7.4 %copy-start.11 = (bf16[1024,512]{0,1:T(8,128)(2,1)S(1)}, bf16[1024,512]{0,1:T(8,128)(2,1)}, u32[]{:S(2)}) copy-start(bf16[1024,512]{0,1:T(8,128)(2,1)} %copy.94) | copy-start | bytes 3145732
  225.9 2.5 copy-start.2
  225.9 3.5 copy-start.7
  347.4 215.1 %all-reduce.3.cloned.1.call-start = ((), (), s32[]{:S(2)}) async-start(), calls=%async_computation.5 | async-start | bytes 10485760 | tf_op jit(solution)/shard_map/psum | solution.py:77
  347.5 3.4 copy-start.3
  562.5 4.8 copy-start.13
Sparse Core Ops, SparseCore 0:
  347.5 83.8 reduce-scatter.3
Sparse Core Ops, SparseCore 1:
  355.6 206.8 all-reduce.2
where the time goes:
time: 581 us; the launch traced here: 576 us
  waiting for transfers between devices  247 us (43%)
  local copies, waits for them, and re-layouts  102 us (18%)
  matrix products  71.9 us (12%)
  other arithmetic  70.6 us (12%)
  blocking collectives  63.3 us (11%)
  between operations  16.3 us (3%)
    psum x1, waiting for transfers between devices, shards(): lax.psum((grad_first.astype(jnp.float32), grad_second.astype(jnp.float32)...  128 us
    unnamed x3, waiting for transfers between devices  72.9 us
    all_to_all x1, blocking collectives, shards(): lax.all_to_all(sending, 'table', split_axis=0, concat_axis=0, tiled=True)  53.6 us
    all_to_all x1, waiting for transfers between devices, shards(): lax.all_to_all(found, 'table', split_axis=0, concat_axis=0, tiled=True)  46 us
    scatter-add x1, other arithmetic, shards(): jax.ops.segment_sum(received.reshape(owners * capacity, width).astype(jnp...  31.7 us
    dot_general x3, matrix products, hstu_layer(): jnp.einsum('thd,shd->hts', query_heads, key_heads, preferred_element_type...  25.3 us
    dot_general x3, matrix products, hstu_layer(): jnp.einsum('hts,shd->thd', weights, value_heads, preferred_element_type=j...  24 us
    unnamed x39, local copies, waits for them, and re-layouts  21.3 us
  transfers between devices with their start and end apart: 3, of which 3 were waited for; matrix products, arithmetic and copies ran while one was open for 3% of the time, Pallas kernels for 0%

commit v1 on v0

--- a/solution.py
+++ b/solution.py
@@ -41,31 +41,44 @@
     )
 
 
+def slot_onehot(place, capacity):
+    events, owners = place.shape
+    spots = lax.broadcasted_iota(jnp.int32, (events, owners, capacity), 2)
+    return (place[:, :, None] == spots).astype(jnp.bfloat16).reshape(events, owners * capacity)
+
+
 def shards(table, w_in, w_out, owner, local_row, doc_ids, out_grad):
     events, lookups_each = owner.shape
     width = table.shape[1]
     rows_owned = table.shape[0]
     owners = lax.axis_size("table")
     capacity = 2 * events * lookups_each // owners
-    lookups = events * lookups_each
-    flat_owner = owner.reshape(lookups)
-    flat_local = local_row.reshape(lookups)
-    member = (flat_owner[:, None] == jnp.arange(owners, dtype=jnp.int32)[None, :]).astype(jnp.int32)
-    position = jnp.sum(jnp.cumsum(member, axis=0) * member, axis=1) - 1
-    slot_index = flat_owner * capacity + position
-    requests = (
-        jnp.zeros((owners * capacity,), jnp.int32)
-        .at[slot_index]
-        .set(flat_local)
-        .reshape(owners, capacity)
+    hits = owner[:, :, None] == jnp.arange(owners, dtype=jnp.int32)[None, None, :]
+    member = jnp.sum(hits.astype(jnp.int32), axis=1)
+    wanted = jnp.sum(jnp.where(hits, local_row[:, :, None], 0), axis=1)
+    earlier = lax.broadcasted_iota(jnp.int32, (events, events), 0) > lax.broadcasted_iota(
+        jnp.int32, (events, events), 1
     )
-    found = jnp.take(
-        table, lax.all_to_all(requests, "table", split_axis=0, concat_axis=0, tiled=True), axis=0
+    before = jnp.dot(
+        earlier.astype(jnp.bfloat16),
+        member.astype(jnp.bfloat16),
+        preferred_element_type=jnp.float32,
+    ).astype(jnp.int32)
+    place = jnp.where(member > 0, before, -1)
+    spots = lax.broadcasted_iota(jnp.int32, (owners, capacity, events), 1)
+    requests = jnp.sum(
+        jnp.where(place.T[:, None, :] == spots, wanted.T[:, None, :], 0), axis=2
     )
-    arrived = lax.all_to_all(found, "table", split_axis=0, concat_axis=0, tiled=True)
-    picked = jnp.take(arrived.reshape(owners * capacity, width), slot_index, axis=0)
-    embedded = jnp.sum(
-        picked.astype(jnp.float32).reshape(events, lookups_each, width), axis=1
+    asked = lax.all_to_all(requests, "table", split_axis=0, concat_axis=0, tiled=True)
+    asked_flat = asked.reshape(owners * capacity)
+    rows = lax.broadcasted_iota(jnp.int32, (owners * capacity, rows_owned), 1)
+    select = (asked_flat[:, None] == rows).astype(jnp.bfloat16)
+    found = jnp.dot(select, table, preferred_element_type=jnp.float32).astype(jnp.bfloat16)
+    arrived = lax.all_to_all(
+        found.reshape(owners, capacity, width), "table", split_axis=0, concat_axis=0, tiled=True
+    ).reshape(owners * capacity, width)
+    embedded = jnp.dot(
+        slot_onehot(place, capacity), arrived, preferred_element_type=jnp.float32
     ).astype(jnp.bfloat16)
     segment = doc_ids[0]
 
@@ -73,32 +86,29 @@
         return hstu_layer(first, second, third, segment)
 
     layer_out, pullback = jax.vjp(forward, embedded, w_in, w_out)
-    embed_grad, grad_first, grad_second = pullback(out_grad)
-    grad_w_in, grad_w_out = lax.psum(
-        (grad_first.astype(jnp.float32), grad_second.astype(jnp.float32)), ("dp", "table")
-    )
-    per_lookup = jnp.broadcast_to(embed_grad[:, None, :], (events, lookups_each, width)).reshape(
-        lookups, width
-    )
-    sending = (
-        jnp.zeros((owners * capacity, width), jnp.bfloat16)
-        .at[slot_index]
-        .set(per_lookup)
-        .reshape(owners, capacity, width)
-    )
-    received, received_ids = (
-        lax.all_to_all(sending, "table", split_axis=0, concat_axis=0, tiled=True),
-        lax.all_to_all(requests, "table", split_axis=0, concat_axis=0, tiled=True),
-    )
-    summed = jax.ops.segment_sum(
-        received.reshape(owners * capacity, width).astype(jnp.float32),
-        received_ids.reshape(-1),
-        num_segments=rows_owned,
-    )
+    embed_grad, grad_first, grad_second = lax.optimization_barrier(pullback(out_grad))
+    grad_w_in, grad_w_out = lax.psum((grad_first, grad_second), ("dp", "table"))
+    sending = lax.dot_general(
+        slot_onehot(place, capacity),
+        embed_grad,
+        (((0,), (0,)), ((), ())),
+        preferred_element_type=jnp.float32,
+    ).astype(jnp.bfloat16)
+    received = lax.all_to_all(
+        sending.reshape(owners, capacity, width), "table", split_axis=0, concat_axis=0, tiled=True
+    ).reshape(owners * capacity, width)
+    lines = lax.broadcasted_iota(jnp.int32, (rows_owned, owners * capacity), 0)
+    spread = (asked_flat[None, :] == lines).astype(jnp.bfloat16)
+    summed = jnp.dot(spread, received, preferred_element_type=jnp.float32)
     grad_table = lax.psum_scatter(
         summed.astype(jnp.bfloat16), "dp", scatter_dimension=1, tiled=True
     ).astype(jnp.float32)
-    return (layer_out, grad_w_in, grad_w_out, grad_table)
+    return (
+        layer_out,
+        grad_w_in.astype(jnp.float32),
+        grad_w_out.astype(jnp.float32),
+        grad_table,
+    )
 
 
 def solution(mesh):

time: 581 us -> 458 us (0.79)
  matrix products: 71.9 us -> 138 us
  local copies, waits for them, and re-layouts: 102 us -> 39.1 us
  blocking collectives: 63.3 us -> 9.72 us
  other arithmetic: 70.6 us -> 29.2 us
  waiting for transfers between devices: 247 us -> 208 us
    unnamed x3, waiting for transfers between devices: 72.9 us -> 0.7 us
    dot_general x0 -> x5, matrix products: none -> 69 us  [the longest x1 28.2 us: shards(): summed = jnp.dot(spread, received, preferred_element_type=jnp.float32)]
    all_to_all x1 -> x0, blocking collectives: 53.6 us -> none  [shards(): lax.all_to_all(sending, 'table', split_axis=0, concat_axis=0, tiled=True)]
    all_to_all x1 -> x2, waiting for transfers between devices: 46 us -> 95.8 us  [the longest x1 53.6 us: shards(): lax.all_to_all(sending.reshape(owners, capacity, width), 'table', split_a...]
    gather x3 -> x0, local copies, waits for them, and re-layouts: 36.3 us -> none  [the longest x1 20.2 us: shards(): jnp.take(table, lax.all_to_all(requests, 'table', split_axis=0, concat_ax...]
    scatter-add x1 -> x0, other arithmetic: 31.7 us -> none  [shards(): jax.ops.segment_sum(received.reshape(owners * capacity, width).astype(jnp...]
    scatter x2 -> x0, local copies, waits for them, and re-layouts: 20.9 us -> none  [the longest x1 12.8 us: shards(): sending = jnp.zeros((owners * capacity, width), jnp.bfloat16).at[slot_ind...]
    psum x1, waiting for transfers between devices: 128 us -> 112 us  [shards(): grad_w_in, grad_w_out = lax.psum((grad_first, grad_second), ('dp', 'table'))]
  transfers between devices with their start and end apart: 3 -> 4, of which waited for: 3 -> 3; matrix products, arithmetic and copies ran while one was open for 3% -> 12% of each run, Pallas kernels for 0% -> 0%
where the time goes in v1:
time: 458 us; the launch traced here: 450 us
  waiting for transfers between devices  208 us (45%)
  matrix products  138 us (30%)
  local copies, waits for them, and re-layouts  39.1 us (9%)
  other arithmetic  29.2 us (6%)
  between operations  16.2 us (4%)
  starting transfers between devices  9.76 us (2%)
  blocking collectives  9.72 us (2%)
    psum x1, waiting for transfers between devices, shards(): grad_w_in, grad_w_out = lax.psum((grad_first, grad_second), ('dp', 'table'))  112 us
    all_to_all x1, waiting for transfers between devices, shards(): lax.all_to_all(sending.reshape(owners, capacity, width), 'table', split_a...  53.6 us
    all_to_all x1, waiting for transfers between devices, shards(): lax.all_to_all(found.reshape(owners, capacity, width), 'table', split_axi...  42.2 us
    dot_general x1, matrix products, shards(): summed = jnp.dot(spread, received, preferred_element_type=jnp.float32)  28.2 us
    dot_general x1, matrix products, shards(): jnp.dot(select, table, preferred_element_type=jnp.float32)  27.4 us
    dot_general x3, matrix products, hstu_layer(): jnp.einsum('thd,shd->hts', query_heads, key_heads, preferred_element_type...  25.3 us
    dot_general x3, matrix products, hstu_layer(): jnp.einsum('hts,shd->thd', weights, value_heads, preferred_element_type=j...  24 us
    unnamed x41, local copies, waits for them, and re-layouts  18.4 us
  transfers between devices with their start and end apart: 4, of which 3 were waited for; matrix products, arithmetic and copies ran while one was open for 12% of the time, Pallas kernels for 0%

profile of v1, /device:TPU:0, one launch (start us, length us, event | category | flops | bytes accessed | tf_op | source)
XLA Modules:
  0.0 450.3 jit_solution(12618570135753470988)
XLA Ops:
  11.4 9.7 %all_to_all.19 = s32[8,1,512]{2,1,0:T(1,128)S(1)} all-to-all(s32[8,1,512]{2,1,0:T(1,128)S(1)} %copy.70), channel_id=1, replica_groups=mesh['dp'=4,'table'=8] {'table'}, dimensions={0} | all-to-all | bytes 32768 | tf_op jit(solution)/shard_map/all_to_all | solution.py:72
  21.2 27.4 %fusion.12 = bf16[4096,512]{1,0:T(8,128)(2,1)} fusion(bf16[4096,512]{1,0:T(8,128)(2,1)} %param.7, s32[4096]{0:T(1024)S(1)} %bitcast.105), kind=kOutput, calls=%fused_computation.27 | convolution fusion | flops 17198743552 | bytes 8404992 | tf_op jit(solution)/shard_map/dot_general | solution.py:76
  48.6 6.5 %copy.71 = bf16[8,512,512]{1,2,0:T(8,128)(2,1)} copy(bf16[8,512,512]{2,1,0:T(8,128)(2,1)} %bitcast.92) | data formatting | bytes 8388608 | tf_op jit(solution)/shard_map/reshape | solution.py:78
  55.1 5.1 %all-to-all-start.1 = ((bf16[8,512,512]{1,2,0:T(8,128)(2,1)}), bf16[8,512,512]{1,2,0:T(8,128)(2,1)}, u32[]{:S(2)}, u32[]{:S(2)}) async-start(bf16[8,512,512]{1,2,0:T(8,128)(2,1)} %copy.71), calls=%async_computation.1 | async-start | bytes 8388608 | tf_op jit(solution)/shard_map/all_to_all | solution.py:77
  61.6 4.0 bitcast_compare_fusion
  67.2 42.2 %all-to-all-done.1 = bf16[8,512,512]{1,2,0:T(8,128)(2,1)} async-done(((bf16[8,512,512]{1,2,0:T(8,128)(2,1)}), bf16[8,512,512]{1,2,0:T(8,128)(2,1)}, u32[]{:S(2)}, u32[]{:S(2)}) %all-to-all-start.1) | async-done | bytes 4194336 | tf_op jit(solution)/shard_map/all_to_all | solution.py:77
  109.4 6.9 %convert_reduce_fusion = (f32[1024]{0:T(1024)S(1)}, bf16[1024,512]{0,1:T(8,128)(2,1)S(1)}) fusion(bf16[8,512,512]{1,2,0:T(8,128)(2,1)} %all-to-all-done.1, s32[1024,8]{0,1:T(8,128)S(1)} %fusion.33), kind=kOutput, calls=%fused_computation.36 | convolution fusion | flops 4300733440 | bytes 5279744 | tf_op jit(solution)/shard_map/dot_general | solution.py:80
  116.6 5.8 %multiply_convert_fusion.1 = (bf16[1024,2048]{1,0:T(8,128)(2,1)S(1)}, f32[1024,2048]{1,0:T(8,128)}) fusion(bf16[512,2048]{1,0:T(8,128)(2,1)S(1)} %copy-done, bf16[1024,512]{0,1:T(8,128)(2,1)S(1)} %get-tuple-element.40, f32[1024]{0:T(1024)S(1)} %fusion.43, f32[1024]{0:T(1024)S(1)} %broadcast_multiply_fusion.1), kind=kOutput, calls=%fused_computation.22 | convolution fusion | flops 2160066560 | bytes 15736832 | tf_op jit(solution)/shard_map/jvp()/dot_general | solution.py:21
  130.7 12.3 %multiply_convert_fusion = (bf16[4,1024,1024]{2,1,0:T(8,128)(2,1)S(1)}, f32[4,1024,1024]{2,1,0:T(8,128)}) fusion(pred[1024,1024]{1,0:T(8,128)(4,1)} %fusion.13, bf16[1024,4,128]{0,2,1:T(8,128)(2,1)} %bitcast.93, bf16[1024,4,128]{0,2,1:T(8,128)(2,1)} %bitcast.95), kind=kOutput, calls=%fused_computation.11 | convolution fusion | flops 1107296256 | bytes 28311552 | tf_op jit(solution)/shard_map/jvp(thd,shd->hts)/dot_general | solution.py:28
  150.7 3.4 multiply_reduce_fusion
  154.1 3.5 fusion.45
  157.6 6.1 %fusion.30 = bf16[4,128,1024]{2,1,0:T(8,128)(2,1)} fusion(bf16[4,1024,1024]{2,1,0:T(8,128)(2,1)} %copy-done.1, f32[1024,512]{1,0:T(8,128)S(1)} %get-tuple-element.31, f32[1024]{0:T(1024)S(1)} %negate_multiply_fusion.1), kind=kOutput, calls=%fused_computation.64 | convolution fusion | flops 1074790400 | bytes 11538432 | tf_op jit(solution)/shard_map/transpose(jvp(hts,shd->thd))/dot_general | solution.py:35
  163.6 15.1 %fusion.6 = bf16[4,1024,1024]{2,1,0:T(8,128)(2,1)} fusion(f32[4,1024,1024]{2,1,0:T(8,128)} %get-tuple-element.44, pred[1024,1024]{1,0:T(8,128)(4,1)S(1)} %copy-done.11, bf16[128,4,8,128]{3,2,1,0:T(8,128)(2,1)S(1)} %copy-done.10, f32[1024,512]{1,0:T(8,128)S(1)} %get-tuple-element.31, f32[1024]{0:T(1024)S(1)} %negate_multiply_fusion.1), kind=kOutput, calls=%fused_computation.9 | convolution fusion | flops 1137704960 | bytes 29364224 | tf_op jit(solution)/shard_map/transpose(jvp(hts,shd->thd))/dot_general | solution.py:35
  178.7 7.4 %fusion.48 = bf16[4,1024,128]{1,2,0:T(8,128)(2,1)} fusion(bf16[4,1024,1024]{2,1,0:T(8,128)(2,1)} %fusion.6, bf16[1024,4,128]{0,2,1:T(8,128)(2,1)S(1)} %bitcast.96), kind=kOutput, calls=%fused_computation.97 | convolution fusion | flops 1073741824 | bytes 10485760 | tf_op jit(solution)/shard_map/transpose(jvp(thd,shd->hts))/dot_general | solution.py:28
  186.1 5.7 %fusion.47 = bf16[4,1024,128]{1,2,0:T(8,128)(2,1)} fusion(bf16[4,1024,1024]{2,1,0:T(8,128)(2,1)} %fusion.6, bf16[1024,4,128]{0,2,1:T(8,128)(2,1)S(1)} %bitcast.94), kind=kOutput, calls=%fused_computation.96 | convolution fusion | flops 1073741824 | bytes 10485760 | tf_op jit(solution)/shard_map/transpose(jvp(thd,shd->hts))/dot_general | solution.py:28
  198.5 6.8 %fusion.8 = bf16[1024,2048]{1,0:T(8,128)(2,1)S(1)} fusion(f32[1024,2048]{1,0:T(8,128)} %get-tuple-element.42, bf16[1024,512]{1,0:T(8,128)(2,1)} %copy.98, bf16[1024,512]{1,0:T(8,128)(2,1)} %copy.97, bf16[1024,512]{1,0:T(8,128)(2,1)} %copy.96, bf16[1024,512]{1,0:T(8,128)(2,1)} %get-tuple-element.36), kind=kLoop, calls=%fused_computation.20 | loop fusion | flops 37748736 | bytes 16777216 | tf_op jit(solution)/shard_map/transpose(jvp(jit(silu)))/add_any | solution.py:21
  205.3 3.7 convolution_convert_fusion.1
  217.3 6.1 %convolution_convert_fusion = bf16[4096,512]{1,0:T(8,128)(2,1)} fusion(pred[1024,4096]{0,1:T(32,128)(4,1)S(1)} %copy-done.5, bf16[1024,512]{0,1:T(8,128)(2,1)S(1)} %add_convert_fusion), kind=kOutput, calls=%fused_computation.26 | convolution fusion | flops 4297064448 | bytes 9437184 | tf_op jit(solution)/shard_map/dot_general | solution.py:91
  223.4 4.5 %all-to-all-start.2 = ((bf16[8,512,512]{2,1,0:T(8,128)(2,1)}), bf16[8,512,512]{2,1,0:T(8,128)(2,1)}, u32[]{:S(2)}, u32[]{:S(2)}) async-start(bf16[8,512,512]{2,1,0:T(8,128)(2,1)} %bitcast.91), calls=%async_computation.2 | async-start | bytes 8388608 | tf_op jit(solution)/shard_map/all_to_all | solution.py:97
  228.7 53.6 %all-to-all-done.2 = bf16[8,512,512]{2,1,0:T(8,128)(2,1)} async-done(((bf16[8,512,512]{2,1,0:T(8,128)(2,1)}), bf16[8,512,512]{2,1,0:T(8,128)(2,1)}, u32[]{:S(2)}, u32[]{:S(2)}) %all-to-all-start.2) | async-done | bytes 4194336 | tf_op jit(solution)/shard_map/all_to_all | solution.py:97
  282.4 28.2 %fusion.11 = bf16[4096,512]{1,0:T(8,128)(2,1)} fusion(bf16[4096,512]{1,0:T(8,128)(2,1)} %bitcast.20, s32[4096]{0:T(1024)S(1)} %bitcast.106), kind=kOutput, calls=%fused_computation.25 | convolution fusion | flops 17198743552 | bytes 8404992 | tf_op jit(solution)/shard_map/dot_general | solution.py:102
  310.6 6.4 %copy.99 = bf16[4096,512]{0,1:T(8,128)(2,1)} copy(bf16[4096,512]{1,0:T(8,128)(2,1)} %fusion.11) | data formatting | bytes 8388608
  322.4 111.6 %all-reduce.3.cloned.1.call-done = (bf16[512,2048]{1,0:T(8,128)(2,1)}, bf16[512,512]{1,0:T(8,128)(2,1)}) async-done(((bf16[512,2048]{1,0:T(8,128)(2,1)}, bf16[512,512]{1,0:T(8,128)(2,1)}), (bf16[512,2048]{1,0:T(8,128)(2,1)}, bf16[512,512]{1,0:T(8,128)(2,1)})) %all-reduce.3.cloned.1.call-update) | async-done | bytes 2621456 | tf_op jit(solution)/shard_map/psum | solution.py:90
  434.0 4.2 convert_element_type.142
  (73 shorter events, 48.1 us)
Async XLA Ops:
  8.0 108.6 %copy-start = (bf16[512,2048]{1,0:T(8,128)(2,1)S(1)}, bf16[512,2048]{1,0:T(8,128)(2,1)}, u32[]{:S(2)}) copy-start(bf16[512,2048]{1,0:T(8,128)(2,1)} %param.8) | copy-start | bytes 6291460
  55.1 5.1 %copy-start.6 = (bf16[1024,512]{1,0:T(8,128)(2,1)S(1)}, bf16[1024,512]{1,0:T(8,128)(2,1)}, u32[]{:S(2)}) copy-start(bf16[1024,512]{1,0:T(8,128)(2,1)} %param.13) | copy-start | bytes 3145732
  55.1 54.3 %all-to-all-start.1 = ((bf16[8,512,512]{1,2,0:T(8,128)(2,1)}), bf16[8,512,512]{1,2,0:T(8,128)(2,1)}, u32[]{:S(2)}, u32[]{:S(2)}) async-start(bf16[8,512,512]{1,2,0:T(8,128)(2,1)} %copy.71), calls=%async_computation.1 | async-start | bytes 8388608 | tf_op jit(solution)/shard_map/all_to_all | solution.py:77
  60.3 5.4 %copy-start.16 = (s32[1,1024]{1,0:T(1,128)S(1)}, s32[1,1024]{1,0:T(1,128)}, u32[]{:S(2)}) copy-start(s32[1,1024]{1,0:T(1,128)} %param.12) | copy-start | bytes 12292
  122.4 2.0 copy-start.4
  130.7 12.3 %copy-start.9 = (bf16[128,4,8,128]{3,2,1,0:T(8,128)(2,1)S(1)}, bf16[128,4,8,128]{3,2,1,0:T(8,128)(2,1)}, u32[]{:S(2)}) copy-start(bf16[128,4,8,128]{3,2,1,0:T(8,128)(2,1)} %get-tuple-element.33) | copy-start | bytes 3145732
  143.0 3.2 copy-start.1
  146.2 1.3 copy-start.3
  150.7 3.4 copy-start.2
  157.6 6.1 %copy-start.10 = (bf16[128,4,8,128]{3,2,1,0:T(8,128)(2,1)S(1)}, bf16[128,4,8,128]{3,2,1,0:T(8,128)(2,1)}, u32[]{:S(2)}) copy-start(bf16[128,4,8,128]{3,2,1,0:T(8,128)(2,1)} %get-tuple-element.33) | copy-start | bytes 3145732
  157.6 6.1 %copy-start.11 = (pred[1024,1024]{1,0:T(8,128)(4,1)S(1)}, pred[1024,1024]{1,0:T(8,128)(4,1)}, u32[]{:S(2)}) copy-start(pred[1024,1024]{1,0:T(8,128)(4,1)} %fusion.13) | copy-start | bytes 3145732
  163.6 15.1 %copy-start.13 = (bf16[1024,512]{0,1:T(8,128)(2,1)S(1)}, bf16[1024,512]{0,1:T(8,128)(2,1)}, u32[]{:S(2)}) copy-start(bf16[1024,512]{0,1:T(8,128)(2,1)} %copy.102) | copy-start | bytes 3145732
  178.7 7.4 %copy-start.12 = (bf16[1024,512]{0,1:T(8,128)(2,1)S(1)}, bf16[1024,512]{0,1:T(8,128)(2,1)}, u32[]{:S(2)}) copy-start(bf16[1024,512]{0,1:T(8,128)(2,1)} %copy.101) | copy-start | bytes 3145732
  209.0 3.9 copy-start.7
  209.0 4.0 copy-start.14
  211.4 1.0 copy-start.8
  214.5 2.8 copy-start.5
  223.4 59.0 %all-to-all-start.2 = ((bf16[8,512,512]{2,1,0:T(8,128)(2,1)}), bf16[8,512,512]{2,1,0:T(8,128)(2,1)}, u32[]{:S(2)}, u32[]{:S(2)}) async-start(bf16[8,512,512]{2,1,0:T(8,128)(2,1)} %bitcast.91), calls=%async_computation.2 | async-start | bytes 8388608 | tf_op jit(solution)/shard_map/all_to_all | solution.py:97
  228.0 206.0 %all-reduce.3.cloned.1.call-start = ((), (), s32[]{:S(2)}) async-start(), calls=%async_computation.5 | async-start | bytes 5242880 | tf_op jit(solution)/shard_map/psum | solution.py:90
  228.7 210.6 %reduce-scatter.4.cloned.1.call-start = ((), (), s32[]{:S(2)}) async-start(), calls=%async_computation.4 | async-start | bytes 5242880
  434.0 4.2 copy-start.15
Sparse Core Ops, SparseCore 0:
  234.8 199.1 all-reduce.2
Sparse Core Ops, SparseCore 1:
  317.1 77.0 reduce-scatter.3

commit v2 on v1

--- a/solution.py
+++ b/solution.py
@@ -1,6 +1,8 @@
 import jax
 import jax.numpy as jnp
 from jax import lax
+from jax.experimental import pallas as pl
+from jax.experimental.pallas import tpu as pltpu
 from jax.sharding import PartitionSpec as P
 
 HEADS = 4
@@ -47,6 +49,70 @@
     return (place[:, :, None] == spots).astype(jnp.bfloat16).reshape(events, owners * capacity)
 
 
+def pick_body(ids_ref, table_ref, out_ref):
+    cells = lax.broadcasted_iota(jnp.int32, (ids_ref.shape[0], table_ref.shape[0]), 1)
+    hit = (ids_ref[...] == cells).astype(jnp.bfloat16)
+    out_ref[...] = jnp.dot(hit, table_ref[...], preferred_element_type=jnp.float32).astype(
+        out_ref.dtype
+    )
+
+
+def add_body(ids_ref, values_ref, out_ref):
+    parts, block, chunk = out_ref.shape
+    first = pl.program_id(0) * block
+    cells = first + lax.broadcasted_iota(jnp.int32, (block, values_ref.shape[0]), 0)
+    hit = (ids_ref[...] == cells).astype(jnp.bfloat16)
+    total = jnp.dot(hit, values_ref[...], preferred_element_type=jnp.float32)
+    for part in range(parts):
+        out_ref[part] = total[:, part * chunk : (part + 1) * chunk].astype(out_ref.dtype)
+
+
+def block_of(size):
+    return 256 if size % 256 == 0 else size
+
+
+def pick_rows(ids, table):
+    count, (rows, width) = ids.shape[0], table.shape
+    block = block_of(count)
+    return pl.pallas_call(
+        pick_body,
+        out_shape=jax.ShapeDtypeStruct((count, width), jnp.bfloat16),
+        grid=(count // block,),
+        in_specs=[
+            pl.BlockSpec((block, 1), lambda i: (i, 0)),
+            pl.BlockSpec((rows, width), lambda i: (0, 0)),
+        ],
+        out_specs=pl.BlockSpec((block, width), lambda i: (i, 0)),
+        compiler_params=pltpu.CompilerParams(vmem_limit_bytes=40 * 1024 * 1024),
+        cost_estimate=pl.CostEstimate(
+            flops=2 * count * rows * width,
+            bytes_accessed=2 * (count + rows) * width,
+            transcendentals=0,
+        ),
+    )(ids.reshape(count, 1), table)
+
+
+def add_rows(ids, values, rows, parts):
+    count, width = values.shape
+    block = block_of(rows)
+    return pl.pallas_call(
+        add_body,
+        out_shape=jax.ShapeDtypeStruct((parts, rows, width // parts), jnp.bfloat16),
+        grid=(rows // block,),
+        in_specs=[
+            pl.BlockSpec((1, count), lambda i: (0, 0)),
+            pl.BlockSpec((count, width), lambda i: (0, 0)),
+        ],
+        out_specs=pl.BlockSpec((parts, block, width // parts), lambda i: (0, i, 0)),
+        compiler_params=pltpu.CompilerParams(vmem_limit_bytes=40 * 1024 * 1024),
+        cost_estimate=pl.CostEstimate(
+            flops=2 * count * rows * width,
+            bytes_accessed=2 * (count + rows) * width,
+            transcendentals=0,
+        ),
+    )(ids.reshape(1, count), values)
+
+
 def shards(table, w_in, w_out, owner, local_row, doc_ids, out_grad):
     events, lookups_each = owner.shape
     width = table.shape[1]
@@ -71,9 +137,7 @@
     )
     asked = lax.all_to_all(requests, "table", split_axis=0, concat_axis=0, tiled=True)
     asked_flat = asked.reshape(owners * capacity)
-    rows = lax.broadcasted_iota(jnp.int32, (owners * capacity, rows_owned), 1)
-    select = (asked_flat[:, None] == rows).astype(jnp.bfloat16)
-    found = jnp.dot(select, table, preferred_element_type=jnp.float32).astype(jnp.bfloat16)
+    found = pick_rows(asked_flat, table)
     arrived = lax.all_to_all(
         found.reshape(owners, capacity, width), "table", split_axis=0, concat_axis=0, tiled=True
     ).reshape(owners * capacity, width)
@@ -87,7 +151,9 @@
 
     layer_out, pullback = jax.vjp(forward, embedded, w_in, w_out)
     embed_grad, grad_first, grad_second = lax.optimization_barrier(pullback(out_grad))
-    grad_w_in, grad_w_out = lax.psum((grad_first, grad_second), ("dp", "table"))
+    groups = lax.axis_size("dp")
+    terms = jnp.concatenate([grad_first, grad_second], axis=1)
+    partial_sum = lax.psum_scatter(terms, "dp", scatter_dimension=0, tiled=True)
     sending = lax.dot_general(
         slot_onehot(place, capacity),
         embed_grad,
@@ -97,16 +163,28 @@
     received = lax.all_to_all(
         sending.reshape(owners, capacity, width), "table", split_axis=0, concat_axis=0, tiled=True
     ).reshape(owners * capacity, width)
-    lines = lax.broadcasted_iota(jnp.int32, (rows_owned, owners * capacity), 0)
-    spread = (asked_flat[None, :] == lines).astype(jnp.bfloat16)
-    summed = jnp.dot(spread, received, preferred_element_type=jnp.float32)
-    grad_table = lax.psum_scatter(
-        summed.astype(jnp.bfloat16), "dp", scatter_dimension=1, tiled=True
-    ).astype(jnp.float32)
+    partial_sum, received = lax.optimization_barrier((partial_sum, received))
+    pieces = lax.all_to_all(
+        partial_sum.reshape(owners, width // (groups * owners), -1),
+        "table",
+        split_axis=0,
+        concat_axis=0,
+        tiled=True,
+    )
+    piece = jnp.sum(pieces.astype(jnp.float32), axis=0).astype(jnp.bfloat16)
+    column = lax.all_gather(piece, "dp", axis=0, tiled=False)
+    whole = lax.all_gather(column, "table", axis=0, tiled=False)
+    weight_grads = (
+        jnp.swapaxes(whole, 0, 1).reshape(width, terms.shape[1]).astype(jnp.float32)
+    )
+    summed = add_rows(asked_flat, received, rows_owned, groups)
+    grad_table = lax.psum_scatter(summed, "dp", scatter_dimension=0, tiled=True)[0].astype(
+        jnp.float32
+    )
     return (
         layer_out,
-        grad_w_in.astype(jnp.float32),
-        grad_w_out.astype(jnp.float32),
+        weight_grads[:, : w_in.shape[1]],
+        weight_grads[:, w_in.shape[1] :],
         grad_table,
     )
 

time: 458 us -> 430 us (0.939)
  waiting for transfers between devices: 208 us -> 118 us
  blocking collectives: 9.72 us -> 92.5 us
  matrix products: 138 us -> 79.2 us
  Pallas kernels: 0 us -> 41.1 us
  local copies, waits for them, and re-layouts: 39.1 us -> 45.8 us
    psum x1 -> x0, waiting for transfers between devices: 112 us -> none  [shards(): grad_w_in, grad_w_out = lax.psum((grad_first, grad_second), ('dp', 'table'))]
    reduce_scatter x0 -> x2, waiting for transfers between devices: none -> 72.7 us  [the longest x1 72.7 us: shards(): lax.psum_scatter(summed, 'dp', scatter_dimension=0, tiled=True)[0]]
    all_to_all x0 -> x2, blocking collectives: none -> 67.7 us  [the longest x1 52.3 us: shards(): lax.all_to_all(sending.reshape(owners, capacity, width), 'table', split_a...]
    dot_general x2 -> x0, matrix products: 55.6 us -> none  [the longest x1 28.2 us: shards(): summed = jnp.dot(spread, received, preferred_element_type=jnp.float32)]
    all_to_all x1 -> x0, waiting for transfers between devices: 53.6 us -> none  [shards(): lax.all_to_all(sending.reshape(owners, capacity, width), 'table', split_a...]
    pallas_call x0 -> x2, Pallas kernels: none -> 41.1 us  [the longest x1 20.6 us: pick_rows(): pl.pallas_call(pick_body, out_shape=jax.ShapeDtypeStruct((count, width),...]
    all_gather x0 -> x1, blocking collectives: none -> 15.1 us  [shards(): column = lax.all_gather(piece, 'dp', axis=0, tiled=False)]
    unnamed x41 -> x47, local copies, waits for them, and re-layouts: 18.4 us -> 19.1 us
  transfers between devices with their start and end apart: 4 -> 4, of which waited for: 3 -> 3; matrix products, arithmetic and copies ran while one was open for 12% -> 5% of each run, Pallas kernels for 0% -> 5%
where the time goes in v2:
time: 430 us; the launch traced here: 425 us
  waiting for transfers between devices  118 us (27%)
  blocking collectives  92.5 us (22%)
  matrix products  79.2 us (18%)
  local copies, waits for them, and re-layouts  45.8 us (11%)
  Pallas kernels  41.1 us (10%)
  other arithmetic  28.4 us (7%)
  between operations  14.4 us (3%)
  starting transfers between devices  5.38 us (1%)
    reduce_scatter x1, waiting for transfers between devices, shards(): lax.psum_scatter(summed, 'dp', scatter_dimension=0, tiled=True)[0]  72.7 us
    all_to_all x1, blocking collectives, shards(): lax.all_to_all(sending.reshape(owners, capacity, width), 'table', split_a...  52.3 us
    all_to_all x1, waiting for transfers between devices, shards(): lax.all_to_all(found.reshape(owners, capacity, width), 'table', split_axi...  45.6 us
    dot_general x3, matrix products, hstu_layer(): jnp.einsum('thd,shd->hts', query_heads, key_heads, preferred_element_type...  25.3 us
    dot_general x3, matrix products, hstu_layer(): jnp.einsum('hts,shd->thd', weights, value_heads, preferred_element_type=j...  24 us
    pallas_call x1, Pallas kernels, pick_rows(): pl.pallas_call(pick_body, out_shape=jax.ShapeDtypeStruct((count, width),...  20.6 us
    pallas_call x1, Pallas kernels, add_rows(): pl.pallas_call(add_body, out_shape=jax.ShapeDtypeStruct((parts, rows, wid...  20.5 us
    unnamed x47, local copies, waits for them, and re-layouts  19.1 us
  transfers between devices with their start and end apart: 4, of which 3 were waited for; matrix products, arithmetic and copies ran while one was open for 5% of the time, Pallas kernels for 5%

profile of v2, /device:TPU:0, one launch (start us, length us, event | category | flops | bytes accessed | tf_op | source)
XLA Modules:
  0.0 425.2 jit_solution(1756935722501479411)
XLA Ops:
  10.6 9.7 %all_to_all.24 = s32[8,1,512]{2,1,0:T(1,128)S(1)} all-to-all(s32[8,1,512]{2,1,0:T(1,128)S(1)} %copy.95), channel_id=1, replica_groups=mesh['dp'=4,'table'=8] {'table'}, dimensions={0} | all-to-all | bytes 32768 | tf_op jit(solution)/shard_map/all_to_all | solution.py:138
  26.1 20.6 %shard_map.102 = bf16[4096,512]{1,0:T(8,128)(2,1)S(1)} custom-call(s32[4096,1]{1,0:T(8,128)S(1)} %copy-done.4, bf16[4096,512]{1,0:T(8,128)(2,1)S(1)} %copy-done.5), custom_call_target="tpu_custom_call" | custom-call | flops 17179869184 | bytes 8388608 | tf_op jit(solution)/shard_map/pallas_call | solution.py:77
  48.8 6.5 %copy.97 = bf16[8,512,512]{1,2,0:T(8,128)(2,1)} copy(bf16[8,512,512]{2,1,0:T(8,128)(2,1)} %bitcast.96) | data formatting | bytes 8388608 | tf_op jit(solution)/shard_map/reshape | solution.py:142
  55.3 4.7 %all-to-all-start.1 = ((bf16[8,512,512]{1,2,0:T(8,128)(2,1)}), bf16[8,512,512]{1,2,0:T(8,128)(2,1)}, u32[]{:S(2)}, u32[]{:S(2)}) async-start(bf16[8,512,512]{1,2,0:T(8,128)(2,1)} %copy.97), calls=%async_computation.1 | async-start | bytes 8388608 | tf_op jit(solution)/shard_map/all_to_all | solution.py:141
  63.5 45.6 %all-to-all-done.1 = bf16[8,512,512]{1,2,0:T(8,128)(2,1)} async-done(((bf16[8,512,512]{1,2,0:T(8,128)(2,1)}), bf16[8,512,512]{1,2,0:T(8,128)(2,1)}, u32[]{:S(2)}, u32[]{:S(2)}) %all-to-all-start.1) | async-done | bytes 4194336 | tf_op jit(solution)/shard_map/all_to_all | solution.py:141
  109.1 6.9 %convert_reduce_fusion = (f32[1024]{0:T(1024)S(1)}, bf16[1024,512]{0,1:T(8,128)(2,1)S(1)}) fusion(bf16[8,512,512]{1,2,0:T(8,128)(2,1)} %all-to-all-done.1, s32[1024,8]{0,1:T(8,128)S(1)} %fusion.27), kind=kOutput, calls=%fused_computation.29 | convolution fusion | flops 4300733440 | bytes 5279744 | tf_op jit(solution)/shard_map/dot_general | solution.py:144
  116.3 5.8 %multiply_convert_fusion.1 = (bf16[1024,2048]{1,0:T(8,128)(2,1)S(1)}, f32[1024,2048]{1,0:T(8,128)}) fusion(bf16[512,2048]{1,0:T(8,128)(2,1)S(1)} %copy-done, bf16[1024,512]{0,1:T(8,128)(2,1)S(1)} %get-tuple-element.46, f32[1024]{0:T(1024)S(1)} %fusion.37, f32[1024]{0:T(1024)S(1)} %broadcast_multiply_fusion.1), kind=kOutput, calls=%fused_computation.16 | convolution fusion | flops 2160066560 | bytes 15736832 | tf_op jit(solution)/shard_map/jvp()/dot_general | solution.py:23
  130.5 12.3 %multiply_convert_fusion = (bf16[4,1024,1024]{2,1,0:T(8,128)(2,1)S(1)}, f32[4,1024,1024]{2,1,0:T(8,128)}) fusion(pred[1024,1024]{1,0:T(8,128)(4,1)} %fusion.7, bf16[1024,4,128]{0,2,1:T(8,128)(2,1)} %bitcast.106, bf16[1024,4,128]{0,2,1:T(8,128)(2,1)} %bitcast.108), kind=kOutput, calls=%fused_computation.5 | convolution fusion | flops 1107296256 | bytes 28311552 | tf_op jit(solution)/shard_map/jvp(thd,shd->hts)/dot_general | solution.py:30
  142.8 2.9 fusion.40
  147.7 2.9 copy.120
  150.6 3.4 multiply_reduce_fusion
  154.0 3.5 fusion.39
  157.5 6.1 %fusion.24 = bf16[4,128,1024]{2,1,0:T(8,128)(2,1)} fusion(bf16[4,1024,1024]{2,1,0:T(8,128)(2,1)} %copy-done.6, f32[1024,512]{1,0:T(8,128)S(1)} %get-tuple-element.37, f32[1024]{0:T(1024)S(1)} %negate_multiply_fusion.1), kind=kOutput, calls=%fused_computation.58 | convolution fusion | flops 1074790400 | bytes 11538432 | tf_op jit(solution)/shard_map/transpose(jvp(hts,shd->thd))/dot_general | solution.py:37
  163.6 15.1 %fusion.2 = bf16[4,1024,1024]{2,1,0:T(8,128)(2,1)} fusion(f32[4,1024,1024]{2,1,0:T(8,128)} %get-tuple-element.50, pred[1024,1024]{1,0:T(8,128)(4,1)S(1)} %copy-done.15, bf16[128,4,8,128]{3,2,1,0:T(8,128)(2,1)S(1)} %copy-done.14, f32[1024,512]{1,0:T(8,128)S(1)} %get-tuple-element.37, f32[1024]{0:T(1024)S(1)} %negate_multiply_fusion.1), kind=kOutput, calls=%fused_computation.3 | convolution fusion | flops 1137704960 | bytes 29364224 | tf_op jit(solution)/shard_map/transpose(jvp(hts,shd->thd))/dot_general | solution.py:37
  178.6 7.4 %fusion.42 = bf16[4,1024,128]{1,2,0:T(8,128)(2,1)} fusion(bf16[4,1024,1024]{2,1,0:T(8,128)(2,1)} %fusion.2, bf16[1024,4,128]{0,2,1:T(8,128)(2,1)S(1)} %bitcast.109), kind=kOutput, calls=%fused_computation.92 | convolution fusion | flops 1073741824 | bytes 10485760 | tf_op jit(solution)/shard_map/transpose(jvp(thd,shd->hts))/dot_general | solution.py:30
  186.0 5.7 %fusion.41 = bf16[4,1024,128]{1,2,0:T(8,128)(2,1)} fusion(bf16[4,1024,1024]{2,1,0:T(8,128)(2,1)} %fusion.2, bf16[1024,4,128]{0,2,1:T(8,128)(2,1)S(1)} %bitcast.107), kind=kOutput, calls=%fused_computation.91 | convolution fusion | flops 1073741824 | bytes 10485760 | tf_op jit(solution)/shard_map/transpose(jvp(thd,shd->hts))/dot_general | solution.py:30
  198.5 6.8 %fusion.4 = bf16[1024,2048]{1,0:T(8,128)(2,1)S(1)} fusion(f32[1024,2048]{1,0:T(8,128)} %get-tuple-element.48, bf16[1024,512]{1,0:T(8,128)(2,1)} %copy.125, bf16[1024,512]{1,0:T(8,128)(2,1)} %copy.124, bf16[1024,512]{1,0:T(8,128)(2,1)} %copy.123, bf16[1024,512]{1,0:T(8,128)(2,1)} %get-tuple-element.42), kind=kLoop, calls=%fused_computation.14 | loop fusion | flops 37748736 | bytes 16777216 | tf_op jit(solution)/shard_map/transpose(jvp(jit(silu)))/add_any | solution.py:23
  217.6 4.8 %convolution_convert_fusion = bf16[4096,512]{1,0:T(8,128)(2,1)S(1)} fusion(pred[1024,4096]{0,1:T(32,128)(4,1)S(1)} %bitcast_compare_fusion, bf16[1024,512]{0,1:T(8,128)(2,1)S(1)} %copy-done.18), kind=kOutput, calls=%fused_computation.19 | convolution fusion | flops 4297064448 | bytes 9437184 | tf_op jit(solution)/shard_map/dot_general | solution.py:157
  222.5 52.3 %all_to_all.25 = bf16[8,512,512]{2,1,0:T(8,128)(2,1)} all-to-all(bf16[8,512,512]{2,1,0:T(8,128)(2,1)S(1)} %bitcast.103), channel_id=1, replica_groups=mesh['dp'=4,'table'=8] {'table'}, dimensions={0} | all-to-all | bytes 8388608 | tf_op jit(solution)/shard_map/all_to_all | solution.py:163
  274.8 15.3 %all_to_all.26 = bf16[8,16,2560]{2,1,0:T(8,128)(2,1)} all-to-all(bf16[8,16,2560]{2,1,0:T(8,128)(2,1)} %bitcast.112), channel_id=1, replica_groups=mesh['dp'=4,'table'=8] {'table'}, dimensions={0} | all-to-all | bytes 1310720 | tf_op jit(solution)/shard_map/all_to_all | solution.py:167
  291.3 15.1 %all-gather = bf16[64,2560]{1,0:T(8,128)(2,1)} all-gather(bf16[16,2560]{1,0:T(8,128)(2,1)S(1)} %reduce_sum.138), channel_id=2, replica_groups=mesh['dp'=4,'table'=8] {'dp'}, dimensions={0}, use_global_device_ids=true | all-gather | bytes 409600 | tf_op jit(solution)/shard_map/all_gather | solution.py:175
  308.7 20.5 %shard_map.103 = bf16[4,4096,128]{2,1,0:T(8,128)(2,1)S(1)} custom-call(s32[1,4096]{1,0:T(1,128)S(1)} %bitcast.98, bf16[4096,512]{1,0:T(8,128)(2,1)S(1)} %bitcast.95), custom_call_target="tpu_custom_call" | custom-call | flops 17179869184 | bytes 8388608 | tf_op jit(solution)/shard_map/pallas_call | solution.py:98
  331.1 3.1 fusion.18
  343.0 72.7 %reduce-scatter.5.cloned.1.call-done = bf16[1,4096,128]{2,1,0:T(8,128)(2,1)} async-done(((bf16[4,4096,128]{2,1,0:T(8,128)(2,1)}), bf16[1,4096,128]{2,1,0:T(8,128)(2,1)}) %reduce-scatter.5.cloned.1.call-update) | async-done | bytes 1048592 | tf_op jit(solution)/shard_map/reduce_scatter | solution.py:181
  (88 shorter events, 61.2 us)
Async XLA Ops:
  7.2 109.1 %copy-start = (bf16[512,2048]{1,0:T(8,128)(2,1)S(1)}, bf16[512,2048]{1,0:T(8,128)(2,1)}, u32[]{:S(2)}) copy-start(bf16[512,2048]{1,0:T(8,128)(2,1)} %param.8) | copy-start | bytes 6291460
  22.3 1.6 copy-start.4
  23.9 2.2 copy-start.5
  46.7 2.0 copy-start.3
  55.3 5.3 %copy-start.10 = (bf16[1024,512]{1,0:T(8,128)(2,1)S(1)}, bf16[1024,512]{1,0:T(8,128)(2,1)}, u32[]{:S(2)}) copy-start(bf16[1024,512]{1,0:T(8,128)(2,1)} %param.13) | copy-start | bytes 3145732
  55.3 6.6 %copy-start.20 = (s32[1,1024]{1,0:T(1,128)S(1)}, s32[1,1024]{1,0:T(1,128)}, u32[]{:S(2)}) copy-start(s32[1,1024]{1,0:T(1,128)} %param.12) | copy-start | bytes 12292
  55.3 53.8 %all-to-all-start.1 = ((bf16[8,512,512]{1,2,0:T(8,128)(2,1)}), bf16[8,512,512]{1,2,0:T(8,128)(2,1)}, u32[]{:S(2)}, u32[]{:S(2)}) async-start(bf16[8,512,512]{1,2,0:T(8,128)(2,1)} %copy.97), calls=%async_computation.1 | async-start | bytes 8388608 | tf_op jit(solution)/shard_map/all_to_all | solution.py:141
  60.0 214.8 %reduce-scatter.3.cloned.1.call-start = ((), (), s32[]{:S(2)}) async-start(), calls=%async_computation.6 | async-start | bytes 3276800 | tf_op jit(solution)/shard_map/reduce_scatter | solution.py:156
  122.1 2.0 copy-start.9
  130.5 12.3 %copy-start.13 = (bf16[128,4,8,128]{3,2,1,0:T(8,128)(2,1)S(1)}, bf16[128,4,8,128]{3,2,1,0:T(8,128)(2,1)}, u32[]{:S(2)}) copy-start(bf16[128,4,8,128]{3,2,1,0:T(8,128)(2,1)} %get-tuple-element.39) | copy-start | bytes 3145732
  142.8 3.2 copy-start.6
  150.6 3.4 copy-start.7
  157.5 6.1 %copy-start.14 = (bf16[128,4,8,128]{3,2,1,0:T(8,128)(2,1)S(1)}, bf16[128,4,8,128]{3,2,1,0:T(8,128)(2,1)}, u32[]{:S(2)}) copy-start(bf16[128,4,8,128]{3,2,1,0:T(8,128)(2,1)} %get-tuple-element.39) | copy-start | bytes 3145732
  157.5 6.1 %copy-start.15 = (pred[1024,1024]{1,0:T(8,128)(4,1)S(1)}, pred[1024,1024]{1,0:T(8,128)(4,1)}, u32[]{:S(2)}) copy-start(pred[1024,1024]{1,0:T(8,128)(4,1)} %fusion.7) | copy-start | bytes 3145732
  163.6 15.1 %copy-start.17 = (bf16[1024,512]{0,1:T(8,128)(2,1)S(1)}, bf16[1024,512]{0,1:T(8,128)(2,1)}, u32[]{:S(2)}) copy-start(bf16[1024,512]{0,1:T(8,128)(2,1)} %copy.127) | copy-start | bytes 3145732
  178.6 7.4 %copy-start.16 = (bf16[1024,512]{0,1:T(8,128)(2,1)S(1)}, bf16[1024,512]{0,1:T(8,128)(2,1)}, u32[]{:S(2)}) copy-start(bf16[1024,512]{0,1:T(8,128)(2,1)} %copy.126) | copy-start | bytes 3145732
  207.6 3.0 copy-start.11
  207.6 3.0 copy-start.19
  210.0 1.4 copy-start.12
  214.9 121.7 %all-gather.4.cloned.1.call-start = ((), (), s32[]{:S(2)}) async-start(), calls=%async_computation.8 | async-start | bytes 2949120 | tf_op jit(solution)/shard_map/all_gather | solution.py:176
  214.9 2.7 copy-start.18
  306.4 109.2 %reduce-scatter.5.cloned.1.call-start = ((), (), s32[]{:S(2)}) async-start(), calls=%async_computation.7 | async-start | bytes 5242880 | tf_op jit(solution)/shard_map/reduce_scatter | solution.py:181
  306.5 2.2 copy-start.2
  329.2 1.9 copy-start.1
  (1 other events, 1.3 us)
Sparse Core Ops, SparseCore 0:
  215.0 51.4 reduce-scatter.2
  306.6 29.9 all-gather.3
  338.9 76.7 reduce-scatter.4
